TPU v7x, 128 devices: a whole 4x4x4 slice. The times are simulated.
128 devices in a mesh: row: 8 (over y, core), col: 16 (over x, z).
Axes of the slice: x: 4, y: 4, z: 4, core: 2. Of those that a mesh axis runs over, the one named last changes fastest.
Arguments:
- densities: bfloat16 [2, 256, 12288], P(None, 'row', 'col'), may hold values from -6 to 6
- pair_weight: bfloat16 [256], P('row'), may hold values from 0.099609375 to 1
- block_perm: int32 [8, 96], replicated, may hold values from 0 to 95, as said below
- phase_index: int32 [8, 12288], replicated, may hold values from 0 to 7
Outputs:
- chi_sym: float32 [2, 12288, 12288], P(None, 'row', 'col')
Inputs may be any that keep to these rules, and one draw needn't show every extreme that they name: `block_perm`: each row is a permutation of the 96 blocks that maps every aligned group of 12 consecutive blocks onto itself.
All inputs are finite; a program needn't handle non-finite values.
Results may differ from a plain program's by a relative error of at most 0.0033.
Values may be sent and summed in bfloat16 or wider, within the bound.
A program may use at most 192 MiB of HBM per device.

v0:
```python
import functools
import math

import jax
import jax.numpy as jnp
from jax import lax
from jax.experimental import pallas as pl
from jax.experimental.pallas import tpu as pltpu
from jax.sharding import PartitionSpec as P

BLOCK = 128
NS = 8
PAIRS = 256
SHARE = 32
WIDE = 768
GROUP = 1536
GROUP_BLOCKS = 12
COL_BLOCKS = 6
FAR_LAG = 2
GATHER_VMEM = 16 * 2**20
NORM = -1.0 / math.sqrt(NS * PAIRS)
HALF_ROOT = math.sqrt(0.5)
MESH = pl.DeviceIdType.MESH


def gather_kernel(
    d_ref, w_ref, hop_ref, col_ref, wt_ref,
    w_own, c_recv, line_recv, far_recv, sib_recv, mate_recv, w_recv, bulk, sib_send, cross_send,
    mate_send, w_send, local,
):
    row = lax.axis_index("row")
    col = lax.axis_index("col")
    y, k = row // 2, row % 2
    x, z = col // 4, col % 4
    zp, q = z % 2, z // 2
    zo = z + 1 - 2 * zp
    zc = (z + 3 + 2 * zp) % 4

    def dev(xx, yy, zz, kk):
        return (2 * yy + kk, 4 * xx + zz)

    on_line = q == k
    is_root = x == y
    to_sib = dev(x, y, z, 1 - k)
    to_zo = dev(x, y, zo, k)
    to_cross = dev(x, y, zc, q)

    def rows_of(yy, kk):
        return pl.ds(pl.multiple_of((2 * yy + kk) * SHARE, SHARE), SHARE)

    def pair_of(yy):
        return pl.ds(pl.multiple_of(yy * 2 * SHARE, 2 * SHARE), 2 * SHARE)

    def cols_of(zz):
        return pl.ds(pl.multiple_of(zz * WIDE, WIDE), WIDE)

    get_w = pltpu.make_async_copy(w_ref, w_own, local.at[1])
    get_w.start()
    keep = pltpu.make_async_copy(d_ref, col_ref.at[:, rows_of(y, k), cols_of(zp)], local.at[0])
    keep.start()

    barrier = pltpu.get_barrier_semaphore()

    def greet(target):
        pl.semaphore_signal(barrier, inc=1, device_id=target, device_id_type=MESH)

    for step in range(1, 8):
        greet(((row + step) % 8, col))
    greet(to_zo)

    @pl.when(jnp.logical_not(is_root))
    def _():
        for yy in range(4):
            greet(dev(y, yy, z, k))

    @pl.when(jnp.logical_not(on_line))
    def _():
        greet(dev(x, y, zc, 0))
        greet(dev(x, y, zc, 1))

    pl.semaphore_wait(barrier, 12)

    def copy(src, dst, send, recv, target):
        return pltpu.make_async_remote_copy(
            src_ref=src, dst_ref=dst, send_sem=send, recv_sem=recv, device_id=target, device_id_type=MESH
        )

    def c_at(yy, zz):
        return col_ref.at[:, rows_of(yy, k), cols_of(zz)]

    def r_at(which, yy, zz):
        return hop_ref.at[which, :, rows_of(yy, k), cols_of(zz)]

    def c_copy(yy, zz, target, src=None):
        there = c_at(yy, zz)
        return copy(there if src is None else src, there, bulk.at[0], c_recv.at[2 * yy + zz], target)

    def spread_block(zz, src):
        for step in range(1, 4):
            target = dev((x + step) % 4, x, z, k)
            copy(src, r_at(q, y, zz), bulk.at[0], line_recv.at[2 * y + zz], target).start()
        for step in range(4):
            yy = (x + step) % 4

            @pl.when(yy != y)
            def _():
                c_copy(y, zz, dev(x, yy, z, k), src).start()

    c_copy(y, zp, to_zo, d_ref).start()
    spread_block(zp, d_ref)
    keep.wait()
    c_copy(y, 1 - zp, to_zo).wait_recv()
    spread_block(1 - zp, c_at(y, 1 - zp))

    def sib_c(yy, kk):
        there = col_ref.at[:, rows_of(yy, kk), :]
        return copy(there, there, sib_send.at[0], sib_recv.at[yy], to_sib)

    sib_c(y, k).start()

    get_w.wait()
    lanes = lax.broadcasted_iota(jnp.int32, (SHARE, SHARE), 1)
    subs = lax.broadcasted_iota(jnp.int32, (SHARE, SHARE), 0)
    spread = jnp.where(lanes == subs, jnp.broadcast_to(w_own[...].astype(jnp.float32), (SHARE, SHARE)), 0.0)
    w_col = jnp.sum(spread, axis=1, keepdims=True)

    def w_at(origin):
        return wt_ref.at[pl.ds(pl.multiple_of(origin * SHARE, SHARE), SHARE), :]

    w_at(row)[...] = jnp.broadcast_to(w_col, (SHARE, BLOCK)).astype(jnp.bfloat16)
    for step in range(1, 8):
        target = ((row + step) % 8, col)
        copy(w_at(row), w_at(row), w_send.at[0], w_recv.at[row], target).start()

    def cross(yy, zz, part, from_col):
        there = hop_ref.at[q, part, rows_of(yy, k), cols_of(zz)]
        src = col_ref.at[part, rows_of(yy, k), cols_of(zz)] if from_col else there
        return copy(src, there, cross_send.at[0], far_recv.at[2 * yy + zz], to_cross)

    def cross_start(yy, zz, from_col):
        @pl.when(zp == 1)
        def _():
            cross(yy, zz, 0, from_col).start()

        @pl.when(zp == 0)
        def _():
            cross(yy, zz, 1, from_col).start()

    def sib_r(yy, zz):
        return copy(r_at(q, yy, zz), r_at(q, yy, zz), sib_send.at[1], sib_recv.at[4], to_sib)

    def line(n):
        yy = (y + n % 4) % 4
        zz = zp if n < 4 else 1 - zp

        @pl.when(is_root)
        def _():
            if n % 4 != 0:
                c_copy(yy, zz, to_zo).wait_recv()
            cross_start(yy, zz, True)
            if n > 4:
                sib_c(yy, k).start()

        @pl.when(jnp.logical_not(is_root))
        def _():
            copy(r_at(q, yy, zz), r_at(q, yy, zz), bulk.at[0], line_recv.at[2 * yy + zz], to_zo).wait_recv()
            cross_start(yy, zz, False)

            @pl.when(jnp.logical_not(on_line))
            def _():
                sib_r(yy, zz).start()

    def mate(yy, zz, part):
        there = hop_ref.at[k, part, pair_of(yy), cols_of(zz)]
        return copy(there, there, mate_send.at[0], mate_recv.at[0], to_zo)

    def far(n):
        yy = (y + n % 4) % 4
        zz = 1 - zp if n < 4 else zp

        def arrive(part):
            there = hop_ref.at[k, part, pair_of(yy), cols_of(zz)]
            copy(there, there, mate_send.at[0], far_recv.at[2 * yy + zz], to_zo).wait_recv()
            mate(yy, zz, part).start()

        @pl.when(jnp.logical_and(jnp.logical_not(on_line), zp == 0))
        def _():
            arrive(0)

        @pl.when(jnp.logical_and(jnp.logical_not(on_line), zp == 1))
        def _():
            arrive(1)

    for step in range(8 + FAR_LAG):
        if step < 8:
            line(step)
        if step >= FAR_LAG:
            far(step - FAR_LAG)

    @pl.when(jnp.logical_not(is_root))
    def _():
        for step in range(1, 4):
            yy = (y + step) % 4
            c_copy(yy, 0, to_zo).wait_recv()
            c_copy(yy, 1, to_zo).wait_recv()
            sib_c(yy, k).start()

    for yy in range(4):
        sib_c(yy, 1 - k).wait_recv()

    half = hop_ref.at[k, :, 0:PAIRS // 2, :]
    whole = hop_ref.at[k, 0]

    @pl.when(jnp.logical_not(on_line))
    def _():
        copy(whole, whole, mate_send.at[0], mate_recv.at[0], to_zo).wait_recv()

    @pl.when(jnp.logical_and(on_line, jnp.logical_not(is_root)))
    def _():
        copy(half, half, sib_send.at[1], sib_recv.at[4], to_sib).wait_recv()

    @pl.when(jnp.logical_and(on_line, is_root))
    def _():
        hop_ref[k] = col_ref[...]

    for step in range(1, 8):
        origin = (row + step) % 8
        copy(w_at(origin), w_at(origin), w_send.at[0], w_recv.at[origin], to_sib).wait_recv()

    sent = col_ref.at[:, 0:208, :]
    copy(sent, sent, bulk.at[0], c_recv.at[0], to_zo).wait_send()
    copy(half, half, sib_send.at[0], sib_recv.at[0], to_sib).wait_send()
    part_half = hop_ref.at[k, 0, 0:PAIRS // 2, :]
    copy(part_half, part_half, cross_send.at[0], far_recv.at[0], to_zo).wait_send()
    w_sent = wt_ref.at[0:7 * SHARE, :]
    copy(w_sent, w_sent, w_send.at[0], w_recv.at[0], to_sib).wait_send()

    @pl.when(jnp.logical_not(on_line))
    def _():
        copy(whole, whole, mate_send.at[0], mate_recv.at[0], to_zo).wait_send()

        @pl.when(jnp.logical_not(is_root))
        def _():
            copy(half, half, sib_send.at[1], sib_recv.at[4], to_sib).wait_send()


def gather(densities, weights):
    vmem = pl.BlockSpec(memory_space=pltpu.VMEM)
    hbm = pl.BlockSpec(memory_space=pltpu.HBM)
    dma = pltpu.SemaphoreType.DMA
    return pl.pallas_call(
        gather_kernel,
        out_shape=[
            jax.ShapeDtypeStruct((2, 2, PAIRS, GROUP), jnp.bfloat16),
            jax.ShapeDtypeStruct((2, PAIRS, GROUP), jnp.bfloat16),
            jax.ShapeDtypeStruct((PAIRS, BLOCK), jnp.bfloat16),
        ],
        in_specs=[hbm, hbm],
        out_specs=[vmem, vmem, vmem],
        scratch_shapes=[
            pltpu.VMEM((1, SHARE), jnp.bfloat16),
            dma((8,)), dma((8,)), dma((8,)), dma((5,)), dma((1,)), dma((8,)), dma((1,)), dma((2,)), dma((1,)),
            dma((1,)), dma((1,)), dma((2,)),
        ],
        compiler_params=pltpu.CompilerParams(
            collective_id=0, has_side_effects=True, vmem_limit_bytes=GATHER_VMEM
        ),
    )(densities, weights)


def turn_parts(phase):
    odd = jnp.where(phase % 2 == 1, HALF_ROOT, 1.0)
    cos_sign = jnp.where(jnp.logical_or(phase < 2, phase == 7), 1.0, jnp.where(jnp.logical_and(phase > 2, phase < 6), -1.0, 0.0))
    sin_sign = jnp.where(jnp.logical_and(phase > 0, phase < 4), 1.0, jnp.where(phase > 4, -1.0, 0.0))
    return cos_sign * odd, sin_sign * odd


def symmetrize_kernel(
    perm_ref, phase_ref, hop_ref, col_ref, wt_ref, out_ref,
    chi, left, right, spread, turns, col_cos, col_sin,
):
    row = lax.axis_index("row")
    col = lax.axis_index("col")
    b = pl.program_id(0)

    @pl.when(b == 0)
    def _():
        entry = lax.broadcasted_iota(jnp.int32, (4 * NS, 2 * NS * BLOCK), 0) % (2 * NS)
        block = lax.broadcasted_iota(jnp.int32, (4 * NS, 2 * NS * BLOCK), 1) // BLOCK
        spread[...] = jnp.where(entry == block, 1.0, 0.0).astype(jnp.bfloat16)

        phases = phase_ref[:, pl.ds(pl.multiple_of(col * WIDE, BLOCK), WIDE)]
        cosine, sine = turn_parts(phases)
        for s in range(NS):
            for c in range(COL_BLOCKS):
                lane = slice(c * BLOCK, (c + 1) * BLOCK)
                col_cos[s, c] = jnp.broadcast_to(cosine[s:s + 1, lane], (8, BLOCK))
                col_sin[s, c] = jnp.broadcast_to(sine[s:s + 1, lane], (8, BLOCK))

        weight = wt_ref[...].astype(jnp.float32) * NORM

        def prepare_left(t, c):
            tile = pl.ds(pl.multiple_of(t * BLOCK, BLOCK), BLOCK)
            for part in range(2):
                scaled = hop_ref[row % 2, part, :, tile].astype(jnp.float32) * weight
                left[tile, part * PAIRS:(part + 1) * PAIRS] = scaled.T.astype(jnp.bfloat16)
            return c

        lax.fori_loop(0, GROUP_BLOCKS, prepare_left, 0, unroll=2)
        right[0:PAIRS, 0:GROUP] = col_ref[0]
        right[PAIRS:2 * PAIRS, 0:GROUP] = col_ref[1]
        right[0:PAIRS, GROUP:2 * GROUP] = -col_ref[1]
        right[PAIRS:2 * PAIRS, GROUP:2 * GROUP] = col_ref[0]

        def multiply(up, c):
            rows = pl.ds(pl.multiple_of(up * 512, 512), 512)
            tile = jnp.dot(left[rows, :], right[...], preferred_element_type=jnp.float32)
            for i in range(4):
                for j in range(2 * GROUP_BLOCKS):
                    chi[up * 4 + i, j] = tile[i * BLOCK:(i + 1) * BLOCK, j * BLOCK:(j + 1) * BLOCK]
            return c

        lax.fori_loop(0, 3, multiply, 0)

    phases = phase_ref[:, pl.ds(pl.multiple_of(row * GROUP + b * BLOCK, BLOCK), BLOCK)]
    both = jnp.concatenate(turn_parts(phases), axis=0)
    coarse = both.astype(jnp.bfloat16).astype(jnp.float32)
    pieces = jnp.concatenate([coarse, both - coarse], axis=0).T.astype(jnp.bfloat16)
    turns[...] = jnp.dot(pieces, spread[...], preferred_element_type=jnp.float32)

    row_from = [perm_ref[s, row * GROUP_BLOCKS + b] - row * GROUP_BLOCKS for s in range(NS)]
    col_group = (col // 2) * GROUP_BLOCKS

    def column(c, carry):
        col_from = [perm_ref[s, col * COL_BLOCKS + c] - col_group for s in range(NS)]
        here = pl.ds(pl.multiple_of(c * BLOCK, BLOCK), BLOCK)

        for t in range(BLOCK // 8):
            rows = slice(t * 8, (t + 1) * 8)
            real = imag = None
            for s in range(NS):
                xr = chi[row_from[s], col_from[s], rows]
                xi = chi[row_from[s], col_from[s] + GROUP_BLOCKS, rows]
                cg = turns[rows, s * BLOCK:(s + 1) * BLOCK]
                sg = turns[rows, (NS + s) * BLOCK:(NS + s + 1) * BLOCK]
                ch, sh = col_cos[s, c], col_sin[s, c]
                turn_c = cg * ch + sg * sh
                turn_s = sg * ch - cg * sh
                add_r = turn_c * xr - turn_s * xi
                add_i = turn_c * xi + turn_s * xr
                real = add_r if s == 0 else real + add_r
                imag = add_i if s == 0 else imag + add_i
            out_ref[0, rows, here] = real
            out_ref[1, rows, here] = imag
        return carry

    lax.fori_loop(0, COL_BLOCKS, column, 0, unroll=2)


def symmetrize(block_perm, phase_index, row_all, col_all, weights):
    vmem = pl.BlockSpec(memory_space=pltpu.VMEM)
    bf16, f32 = jnp.bfloat16, jnp.float32
    return pl.pallas_call(
        symmetrize_kernel,
        grid=(GROUP_BLOCKS,),
        out_shape=jax.ShapeDtypeStruct((2, GROUP, WIDE), f32),
        in_specs=[pl.BlockSpec(memory_space=pltpu.SMEM), vmem, vmem, vmem, vmem],
        out_specs=pl.BlockSpec((2, BLOCK, WIDE), lambda b: (0, b, 0)),
        scratch_shapes=[
            pltpu.VMEM((GROUP_BLOCKS, 2 * GROUP_BLOCKS, BLOCK, BLOCK), f32),
            pltpu.VMEM((GROUP, 2 * PAIRS), bf16),
            pltpu.VMEM((2 * PAIRS, 2 * GROUP), bf16),
            pltpu.VMEM((4 * NS, 2 * NS * BLOCK), bf16),
            pltpu.VMEM((BLOCK, 2 * NS * BLOCK), f32),
            pltpu.VMEM((NS, COL_BLOCKS, 8, BLOCK), f32),
            pltpu.VMEM((NS, COL_BLOCKS, 8, BLOCK), f32),
        ],
        compiler_params=pltpu.CompilerParams(vmem_limit_bytes=48 * 2**20),
    )(block_perm, phase_index, row_all, col_all, weights)


def shards(densities, pair_weight, block_perm, phase_index):
    row_all, col_all, weights = gather(densities, pair_weight.reshape(1, SHARE))
    return symmetrize(block_perm, phase_index, row_all, col_all, weights)


def solution(mesh):
    return jax.shard_map(
        shards,
        mesh=mesh,
        in_specs=(P(None, "row", "col"), P("row"), P(), P()),
        out_specs=P(None, "row", "col"),
        check_vma=False,
    )
```

profile of v0, /device:TPU:1, one launch (start us, length us, event | category | flops | bytes accessed | tf_op | source)
XLA Modules:
  0.0 64.1 jit_solution(16292799481589980229)
XLA Ops:
  0.0 0.0 copy-start.1
  0.0 0.9 %copy-done.1 = bf16[2,32,768]{2,1,0:T(8,128)(2,1)S(1)} copy-done((bf16[2,32,768]{2,1,0:T(8,128)(2,1)S(1)}, bf16[2,32,768]{2,1,0:T(8,128)(2,1)}, u32[]{:S(2)}) %copy-start.1) | copy-done | bytes 98328
  0.9 0.0 copy-start.3
  0.9 0.7 %copy-done.3 = bf16[32]{0:T(256)(128)(2,1)S(1)} copy-done((bf16[32]{0:T(256)(128)(2,1)S(1)}, bf16[32]{0:T(256)(128)(2,1)}, u32[]{:S(2)}) %copy-start.3) | copy-done | bytes 88
  1.5 30.7 %shard_map.46 = (bf16[2,2,256,1536]{3,2,1,0:T(8,128)(2,1)S(1)}, bf16[2,256,1536]{2,1,0:T(8,128)(2,1)S(1)}, bf16[256,128]{1,0:T(8,128)(2,1)S(1)}) custom-call(bf16[2,32,768]{2,1,0:T(8,128)(2,1)S(1)} %copy-done.1, bf16[1,32]{1,0:T(2,128)(2,1)S(1)} %bitcast.1), custom_call_target="tpu_custom_call" | custom-call | tf_op jit(solution)/shard_map/pallas_call | solution.py:251
  32.3 0.0 copy-start
  32.3 1.0 %copy-done = s32[8,12288]{1,0:T(8,128)S(1)} copy-done((s32[8,12288]{1,0:T(8,128)S(1)}, s32[8,12288]{1,0:T(8,128)}, u32[]{:S(2)}) %copy-start) | copy-done | bytes 393240
  33.3 0.0 copy-start.2
  33.3 0.7 %copy-done.2 = s32[8,96]{1,0:T(8,128)S(1)} copy-done((s32[8,96]{1,0:T(8,128)S(1)}, s32[8,96]{1,0:T(8,128)}, u32[]{:S(2)}) %copy-start.2) | copy-done | bytes 3096
  33.9 30.1 %shard_map.47 = f32[2,1536,768]{2,1,0:T(8,128)} custom-call(s32[8,96]{1,0:T(8,128)S(1)} %copy-done.2, s32[8,12288]{1,0:T(8,128)S(1)} %copy-done, bf16[2,2,256,1536]{3,2,1,0:T(8,128)(2,1)S(1)} %get-tuple-element.8.hop_ref, bf16[2,256,1536]{2,1,0:T(8,128)(2,1)S(1)} %get-tuple-element.9.col_ref, bf16[256,128]{1,0:T(8,128)(2,1)S(1)} %get-tuple-element.10.wt_ref), custom_call_target="tpu_custom_call" | custom-call | tf_op jit(solution)/shard_map/pallas_call | solution.py:363
Async XLA Ops:
  0.0 0.9 %copy-start.1 = (bf16[2,32,768]{2,1,0:T(8,128)(2,1)S(1)}, bf16[2,32,768]{2,1,0:T(8,128)(2,1)}, u32[]{:S(2)}) copy-start(bf16[2,32,768]{2,1,0:T(8,128)(2,1)} %d_ref.1) | copy-start | bytes 294916
  0.9 0.7 %copy-start.3 = (bf16[32]{0:T(256)(128)(2,1)S(1)}, bf16[32]{0:T(256)(128)(2,1)}, u32[]{:S(2)}) copy-start(bf16[32]{0:T(256)(128)(2,1)} %param.5) | copy-start | bytes 196
  32.3 1.0 %copy-start = (s32[8,12288]{1,0:T(8,128)S(1)}, s32[8,12288]{1,0:T(8,128)}, u32[]{:S(2)}) copy-start(s32[8,12288]{1,0:T(8,128)} %phase_ref.1) | copy-start | bytes 1179652
  33.3 0.7 %copy-start.2 = (s32[8,96]{1,0:T(8,128)S(1)}, s32[8,96]{1,0:T(8,128)}, u32[]{:S(2)}) copy-start(s32[8,96]{1,0:T(8,128)} %perm_ref.1) | copy-start | bytes 9220
where the time goes:
time: 64.3 us; the launch traced here: 64.1 us
  Pallas kernels  60.8 us (95%)
  local copies, waits for them, and re-layouts  3.22 us (5%)
    pallas_call x1, Pallas kernels, gather(): pl.pallas_call(gather_kernel, out_shape=[jax.ShapeDtypeStruct((2, 2, PAIR...  30.7 us
    pallas_call x1, Pallas kernels, symmetrize(): pl.pallas_call(symmetrize_kernel, grid=(GROUP_BLOCKS,), out_shape=jax.Sha...  30.1 us
    unnamed x8, local copies, waits for them, and re-layouts  3.22 us

commit v1 on v0

--- a/solution.py
+++ b/solution.py
@@ -23,8 +23,15 @@
 MESH = pl.DeviceIdType.MESH
 
 
+def turn_parts(phase):
+    odd = jnp.where(phase % 2 == 1, HALF_ROOT, 1.0)
+    cos_sign = jnp.where(jnp.logical_or(phase < 2, phase == 7), 1.0, jnp.where(jnp.logical_and(phase > 2, phase < 6), -1.0, 0.0))
+    sin_sign = jnp.where(jnp.logical_and(phase > 0, phase < 4), 1.0, jnp.where(phase > 4, -1.0, 0.0))
+    return cos_sign * odd, sin_sign * odd
+
+
 def gather_kernel(
-    d_ref, w_ref, hop_ref, col_ref, wt_ref,
+    d_ref, w_ref, phase_ref, hop_ref, col_ref, wt_ref, row_turns, col_turns,
     w_own, c_recv, line_recv, far_recv, sib_recv, mate_recv, w_recv, bulk, sib_send, cross_send,
     mate_send, w_send, local,
 ):
@@ -108,6 +115,20 @@
 
     c_copy(y, zp, to_zo, d_ref).start()
     spread_block(zp, d_ref)
+
+    cosine, sine = turn_parts(phase_ref[:, pl.ds(pl.multiple_of(col * WIDE, BLOCK), WIDE)])
+    col_turns[0] = cosine
+    col_turns[1] = sine
+
+    def row_block(b, carry):
+        phases = phase_ref[:, pl.ds(pl.multiple_of(row * GROUP + b * BLOCK, BLOCK), BLOCK)]
+        both = jnp.concatenate(turn_parts(phases), axis=0)
+        coarse = both.astype(jnp.bfloat16).astype(jnp.float32)
+        pieces = jnp.concatenate([coarse, both - coarse], axis=0).T.astype(jnp.bfloat16)
+        row_turns[pl.ds(pl.multiple_of(b * BLOCK, BLOCK), BLOCK), :] = pieces
+        return carry
+
+    lax.fori_loop(0, GROUP_BLOCKS, row_block, 0)
     keep.wait()
     c_copy(y, 1 - zp, to_zo).wait_recv()
     spread_block(1 - zp, c_at(y, 1 - zp))
@@ -146,6 +167,9 @@
         def _():
             cross(yy, zz, 1, from_col).start()
 
+    def cross_both(yy, zz):
+        return copy(c_at(yy, zz), r_at(q, yy, zz), cross_send.at[0], far_recv.at[2 * yy + zz], to_cross)
+
     def sib_r(yy, zz):
         return copy(r_at(q, yy, zz), r_at(q, yy, zz), sib_send.at[1], sib_recv.at[4], to_sib)
 
@@ -157,7 +181,10 @@
         def _():
             if n % 4 != 0:
                 c_copy(yy, zz, to_zo).wait_recv()
-            cross_start(yy, zz, True)
+            if n % 4 == 2:
+                cross_both(yy, zz).start()
+            else:
+                cross_start(yy, zz, True)
             if n > 4:
                 sib_c(yy, k).start()
 
@@ -183,11 +210,20 @@
             copy(there, there, mate_send.at[0], far_recv.at[2 * yy + zz], to_zo).wait_recv()
             mate(yy, zz, part).start()
 
-        @pl.when(jnp.logical_and(jnp.logical_not(on_line), zp == 0))
+        relayed = jnp.logical_not(on_line)
+        if n % 4 == 2:
+            @pl.when(jnp.logical_and(relayed, is_root))
+            def _():
+                there = hop_ref.at[k, :, pair_of(yy), cols_of(zz)]
+                copy(there, there, mate_send.at[0], far_recv.at[2 * yy + zz], to_zo).wait_recv()
+
+            relayed = jnp.logical_and(relayed, jnp.logical_not(is_root))
+
+        @pl.when(jnp.logical_and(relayed, zp == 0))
         def _():
             arrive(0)
 
-        @pl.when(jnp.logical_and(jnp.logical_not(on_line), zp == 1))
+        @pl.when(jnp.logical_and(relayed, zp == 1))
         def _():
             arrive(1)
 
@@ -210,8 +246,15 @@
 
     half = hop_ref.at[k, :, 0:PAIRS // 2, :]
     whole = hop_ref.at[k, 0]
-
-    @pl.when(jnp.logical_not(on_line))
+    most = hop_ref.at[k, 0, 0:3 * PAIRS // 4, :]
+    far_root = jnp.logical_and(jnp.logical_not(on_line), is_root)
+    far_other = jnp.logical_and(jnp.logical_not(on_line), jnp.logical_not(is_root))
+
+    @pl.when(far_root)
+    def _():
+        copy(most, most, mate_send.at[0], mate_recv.at[0], to_zo).wait_recv()
+
+    @pl.when(far_other)
     def _():
         copy(whole, whole, mate_send.at[0], mate_recv.at[0], to_zo).wait_recv()
 
@@ -231,20 +274,30 @@
     copy(sent, sent, bulk.at[0], c_recv.at[0], to_zo).wait_send()
     copy(half, half, sib_send.at[0], sib_recv.at[0], to_sib).wait_send()
     part_half = hop_ref.at[k, 0, 0:PAIRS // 2, :]
-    copy(part_half, part_half, cross_send.at[0], far_recv.at[0], to_zo).wait_send()
+    part_more = hop_ref.at[k, 0, 0:5 * PAIRS // 8, :]
+
+    @pl.when(is_root)
+    def _():
+        copy(part_more, part_more, cross_send.at[0], far_recv.at[0], to_zo).wait_send()
+
+    @pl.when(jnp.logical_not(is_root))
+    def _():
+        copy(part_half, part_half, cross_send.at[0], far_recv.at[0], to_zo).wait_send()
+
     w_sent = wt_ref.at[0:7 * SHARE, :]
     copy(w_sent, w_sent, w_send.at[0], w_recv.at[0], to_sib).wait_send()
 
-    @pl.when(jnp.logical_not(on_line))
+    @pl.when(far_root)
+    def _():
+        copy(most, most, mate_send.at[0], mate_recv.at[0], to_zo).wait_send()
+
+    @pl.when(far_other)
     def _():
         copy(whole, whole, mate_send.at[0], mate_recv.at[0], to_zo).wait_send()
-
-        @pl.when(jnp.logical_not(is_root))
-        def _():
-            copy(half, half, sib_send.at[1], sib_recv.at[4], to_sib).wait_send()
-
-
-def gather(densities, weights):
+        copy(half, half, sib_send.at[1], sib_recv.at[4], to_sib).wait_send()
+
+
+def gather(densities, weights, phase_index):
     vmem = pl.BlockSpec(memory_space=pltpu.VMEM)
     hbm = pl.BlockSpec(memory_space=pltpu.HBM)
     dma = pltpu.SemaphoreType.DMA
@@ -254,9 +307,11 @@
             jax.ShapeDtypeStruct((2, 2, PAIRS, GROUP), jnp.bfloat16),
             jax.ShapeDtypeStruct((2, PAIRS, GROUP), jnp.bfloat16),
             jax.ShapeDtypeStruct((PAIRS, BLOCK), jnp.bfloat16),
+            jax.ShapeDtypeStruct((GROUP, 4 * NS), jnp.bfloat16),
+            jax.ShapeDtypeStruct((2, NS, WIDE), jnp.float32),
         ],
-        in_specs=[hbm, hbm],
-        out_specs=[vmem, vmem, vmem],
+        in_specs=[hbm, hbm, vmem],
+        out_specs=[vmem, vmem, vmem, vmem, vmem],
         scratch_shapes=[
             pltpu.VMEM((1, SHARE), jnp.bfloat16),
             dma((8,)), dma((8,)), dma((8,)), dma((5,)), dma((1,)), dma((8,)), dma((1,)), dma((2,)), dma((1,)),
@@ -265,18 +320,11 @@
         compiler_params=pltpu.CompilerParams(
             collective_id=0, has_side_effects=True, vmem_limit_bytes=GATHER_VMEM
         ),
-    )(densities, weights)
-
-
-def turn_parts(phase):
-    odd = jnp.where(phase % 2 == 1, HALF_ROOT, 1.0)
-    cos_sign = jnp.where(jnp.logical_or(phase < 2, phase == 7), 1.0, jnp.where(jnp.logical_and(phase > 2, phase < 6), -1.0, 0.0))
-    sin_sign = jnp.where(jnp.logical_and(phase > 0, phase < 4), 1.0, jnp.where(phase > 4, -1.0, 0.0))
-    return cos_sign * odd, sin_sign * odd
+    )(densities, weights, phase_index)
 
 
 def symmetrize_kernel(
-    perm_ref, phase_ref, hop_ref, col_ref, wt_ref, out_ref,
+    perm_ref, row_turns, col_turns, hop_ref, col_ref, wt_ref, out_ref,
     chi, left, right, spread, turns, col_cos, col_sin,
 ):
     row = lax.axis_index("row")
@@ -289,8 +337,7 @@
         block = lax.broadcasted_iota(jnp.int32, (4 * NS, 2 * NS * BLOCK), 1) // BLOCK
         spread[...] = jnp.where(entry == block, 1.0, 0.0).astype(jnp.bfloat16)
 
-        phases = phase_ref[:, pl.ds(pl.multiple_of(col * WIDE, BLOCK), WIDE)]
-        cosine, sine = turn_parts(phases)
+        cosine, sine = col_turns[0], col_turns[1]
         for s in range(NS):
             for c in range(COL_BLOCKS):
                 lane = slice(c * BLOCK, (c + 1) * BLOCK)
@@ -322,11 +369,8 @@
 
         lax.fori_loop(0, 3, multiply, 0)
 
-    phases = phase_ref[:, pl.ds(pl.multiple_of(row * GROUP + b * BLOCK, BLOCK), BLOCK)]
-    both = jnp.concatenate(turn_parts(phases), axis=0)
-    coarse = both.astype(jnp.bfloat16).astype(jnp.float32)
-    pieces = jnp.concatenate([coarse, both - coarse], axis=0).T.astype(jnp.bfloat16)
-    turns[...] = jnp.dot(pieces, spread[...], preferred_element_type=jnp.float32)
+    mine = row_turns[pl.ds(pl.multiple_of(b * BLOCK, BLOCK), BLOCK), :]
+    turns[...] = jnp.dot(mine, spread[...], preferred_element_type=jnp.float32)
 
     row_from = [perm_ref[s, row * GROUP_BLOCKS + b] - row * GROUP_BLOCKS for s in range(NS)]
     col_group = (col // 2) * GROUP_BLOCKS
@@ -357,14 +401,14 @@
     lax.fori_loop(0, COL_BLOCKS, column, 0, unroll=2)
 
 
-def symmetrize(block_perm, phase_index, row_all, col_all, weights):
+def symmetrize(block_perm, row_turns, col_turns, row_all, col_all, weights):
     vmem = pl.BlockSpec(memory_space=pltpu.VMEM)
     bf16, f32 = jnp.bfloat16, jnp.float32
     return pl.pallas_call(
         symmetrize_kernel,
         grid=(GROUP_BLOCKS,),
         out_shape=jax.ShapeDtypeStruct((2, GROUP, WIDE), f32),
-        in_specs=[pl.BlockSpec(memory_space=pltpu.SMEM), vmem, vmem, vmem, vmem],
+        in_specs=[pl.BlockSpec(memory_space=pltpu.SMEM), vmem, vmem, vmem, vmem, vmem],
         out_specs=pl.BlockSpec((2, BLOCK, WIDE), lambda b: (0, b, 0)),
         scratch_shapes=[
             pltpu.VMEM((GROUP_BLOCKS, 2 * GROUP_BLOCKS, BLOCK, BLOCK), f32),
@@ -376,12 +420,12 @@
             pltpu.VMEM((NS, COL_BLOCKS, 8, BLOCK), f32),
         ],
         compiler_params=pltpu.CompilerParams(vmem_limit_bytes=48 * 2**20),
-    )(block_perm, phase_index, row_all, col_all, weights)
+    )(block_perm, row_turns, col_turns, row_all, col_all, weights)
 
 
 def shards(densities, pair_weight, block_perm, phase_index):
-    row_all, col_all, weights = gather(densities, pair_weight.reshape(1, SHARE))
-    return symmetrize(block_perm, phase_index, row_all, col_all, weights)
+    row_all, col_all, weights, row_turns, col_turns = gather(densities, pair_weight.reshape(1, SHARE), phase_index)
+    return symmetrize(block_perm, row_turns, col_turns, row_all, col_all, weights)
 
 
 def solution(mesh):

time: 64.3 us -> 62.8 us (0.977)
  Pallas kernels: 60.8 us -> 59.4 us
    pallas_call x1, Pallas kernels: 30.1 us -> 29.1 us  [symmetrize(): pl.pallas_call(symmetrize_kernel, grid=(GROUP_BLOCKS,), out_shape=jax.Sha...]
where the time goes in v1:
time: 62.8 us; the launch traced here: 62.6 us
  Pallas kernels  59.4 us (95%)
  local copies, waits for them, and re-layouts  3.22 us (5%)
    pallas_call x1, Pallas kernels, gather(): pl.pallas_call(gather_kernel, out_shape=[jax.ShapeDtypeStruct((2, 2, PAIR...  30.2 us
    pallas_call x1, Pallas kernels, symmetrize(): pl.pallas_call(symmetrize_kernel, grid=(GROUP_BLOCKS,), out_shape=jax.Sha...  29.1 us
    unnamed x8, local copies, waits for them, and re-layouts  3.22 us

profile of v1, /device:TPU:1, one launch (start us, length us, event | category | flops | bytes accessed | tf_op | source)
XLA Modules:
  0.0 62.6 jit_solution(4701891207029743797)
XLA Ops:
  0.0 0.0 copy-start
  0.0 1.0 %copy-done = s32[8,12288]{1,0:T(8,128)S(1)} copy-done((s32[8,12288]{1,0:T(8,128)S(1)}, s32[8,12288]{1,0:T(8,128)}, u32[]{:S(2)}) %copy-start) | copy-done | bytes 393240
  1.0 0.0 copy-start.1
  1.0 0.9 %copy-done.1 = bf16[2,32,768]{2,1,0:T(8,128)(2,1)S(1)} copy-done((bf16[2,32,768]{2,1,0:T(8,128)(2,1)S(1)}, bf16[2,32,768]{2,1,0:T(8,128)(2,1)}, u32[]{:S(2)}) %copy-start.1) | copy-done | bytes 98328
  1.9 0.0 copy-start.3
  1.9 0.7 %copy-done.3 = bf16[32]{0:T(256)(128)(2,1)S(1)} copy-done((bf16[32]{0:T(256)(128)(2,1)S(1)}, bf16[32]{0:T(256)(128)(2,1)}, u32[]{:S(2)}) %copy-start.3) | copy-done | bytes 88
  2.5 30.2 %shard_map.46 = (bf16[2,2,256,1536]{3,2,1,0:T(8,128)(2,1)S(1)}, bf16[2,256,1536]{2,1,0:T(8,128)(2,1)S(1)}, bf16[256,128]{1,0:T(8,128)(2,1)S(1)}, bf16[1536,32]{1,0:T(8,128)(2,1)S(1)}, f32[2,8,768]{2,1,0:T(8,128)S(1)}) custom-call(bf16[2,32,768]{2,1,0:T(8,128)(2,1)S(1)} %copy-done.1, bf16[1,32]{1,0:T(2,128)(2,1)S(1)} %bitcast.1, s32[8,12288]{1,0:T(8,128)S(1)} %copy-done), custom_call_target="tpu_custom_call" | custom-call | tf_op jit(solution)/shard_map/pallas_call | solution.py:304
  32.8 0.0 copy-start.2
  32.8 0.7 %copy-done.2 = s32[8,96]{1,0:T(8,128)S(1)} copy-done((s32[8,96]{1,0:T(8,128)S(1)}, s32[8,96]{1,0:T(8,128)}, u32[]{:S(2)}) %copy-start.2) | copy-done | bytes 3096
  33.5 29.1 %shard_map.47 = f32[2,1536,768]{2,1,0:T(8,128)} custom-call(s32[8,96]{1,0:T(8,128)S(1)} %copy-done.2, bf16[1536,32]{1,0:T(8,128)(2,1)S(1)} %get-tuple-element.10.row_turns, f32[2,8,768]{2,1,0:T(8,128)S(1)} %get-tuple-element.11.col_turns, bf16[2,2,256,1536]{3,2,1,0:T(8,128)(2,1)S(1)} %get-tuple-element.12.hop_ref, ...), custom_call_target="tpu_custom_call" | custom-call | tf_op jit(solution)/shard_map/pallas_call | solution.py:407
Async XLA Ops:
  0.0 1.0 %copy-start = (s32[8,12288]{1,0:T(8,128)S(1)}, s32[8,12288]{1,0:T(8,128)}, u32[]{:S(2)}) copy-start(s32[8,12288]{1,0:T(8,128)} %phase_ref.1) | copy-start | bytes 1179652
  1.0 0.9 %copy-start.1 = (bf16[2,32,768]{2,1,0:T(8,128)(2,1)S(1)}, bf16[2,32,768]{2,1,0:T(8,128)(2,1)}, u32[]{:S(2)}) copy-start(bf16[2,32,768]{2,1,0:T(8,128)(2,1)} %d_ref.1) | copy-start | bytes 294916
  1.9 0.7 %copy-start.3 = (bf16[32]{0:T(256)(128)(2,1)S(1)}, bf16[32]{0:T(256)(128)(2,1)}, u32[]{:S(2)}) copy-start(bf16[32]{0:T(256)(128)(2,1)} %param.5) | copy-start | bytes 196
  32.8 0.7 %copy-start.2 = (s32[8,96]{1,0:T(8,128)S(1)}, s32[8,96]{1,0:T(8,128)}, u32[]{:S(2)}) copy-start(s32[8,96]{1,0:T(8,128)} %perm_ref.1) | copy-start | bytes 9220

commit v2 on v1

--- a/solution.py
+++ b/solution.py
@@ -353,21 +353,21 @@
                 left[tile, part * PAIRS:(part + 1) * PAIRS] = scaled.T.astype(jnp.bfloat16)
             return c
 
-        lax.fori_loop(0, GROUP_BLOCKS, prepare_left, 0, unroll=2)
+        lax.fori_loop(0, GROUP_BLOCKS, prepare_left, 0, unroll=6)
         right[0:PAIRS, 0:GROUP] = col_ref[0]
         right[PAIRS:2 * PAIRS, 0:GROUP] = col_ref[1]
         right[0:PAIRS, GROUP:2 * GROUP] = -col_ref[1]
         right[PAIRS:2 * PAIRS, GROUP:2 * GROUP] = col_ref[0]
 
         def multiply(up, c):
-            rows = pl.ds(pl.multiple_of(up * 512, 512), 512)
+            rows = pl.ds(pl.multiple_of(up * 768, 768), 768)
             tile = jnp.dot(left[rows, :], right[...], preferred_element_type=jnp.float32)
-            for i in range(4):
+            for i in range(6):
                 for j in range(2 * GROUP_BLOCKS):
-                    chi[up * 4 + i, j] = tile[i * BLOCK:(i + 1) * BLOCK, j * BLOCK:(j + 1) * BLOCK]
+                    chi[up * 6 + i, j] = tile[i * BLOCK:(i + 1) * BLOCK, j * BLOCK:(j + 1) * BLOCK]
             return c
 
-        lax.fori_loop(0, 3, multiply, 0)
+        lax.fori_loop(0, 2, multiply, 0)
 
     mine = row_turns[pl.ds(pl.multiple_of(b * BLOCK, BLOCK), BLOCK), :]
     turns[...] = jnp.dot(mine, spread[...], preferred_element_type=jnp.float32)

time: 62.8 us -> 62.4 us (level)
  no operation moved by 1% of the time
where the time goes in v2:
time: 62.4 us; the launch traced here: 62.2 us
  Pallas kernels  58.9 us (94%)
  local copies, waits for them, and re-layouts  3.22 us (5%)
    pallas_call x1, Pallas kernels, gather(): pl.pallas_call(gather_kernel, out_shape=[jax.ShapeDtypeStruct((2, 2, PAIR...  30.2 us
    pallas_call x1, Pallas kernels, symmetrize(): pl.pallas_call(symmetrize_kernel, grid=(GROUP_BLOCKS,), out_shape=jax.Sha...  28.7 us
    unnamed x8, local copies, waits for them, and re-layouts  3.22 us

profile of v2, /device:TPU:1, one launch (start us, length us, event | category | flops | bytes accessed | tf_op | source)
XLA Modules:
  0.0 62.2 jit_solution(5119240549429501787)
XLA Ops:
  0.0 0.0 copy-start
  0.0 1.0 %copy-done = s32[8,12288]{1,0:T(8,128)S(1)} copy-done((s32[8,12288]{1,0:T(8,128)S(1)}, s32[8,12288]{1,0:T(8,128)}, u32[]{:S(2)}) %copy-start) | copy-done | bytes 393240
  1.0 0.0 copy-start.1
  1.0 0.9 %copy-done.1 = bf16[2,32,768]{2,1,0:T(8,128)(2,1)S(1)} copy-done((bf16[2,32,768]{2,1,0:T(8,128)(2,1)S(1)}, bf16[2,32,768]{2,1,0:T(8,128)(2,1)}, u32[]{:S(2)}) %copy-start.1) | copy-done | bytes 98328
  1.9 0.0 copy-start.3
  1.9 0.7 %copy-done.3 = bf16[32]{0:T(256)(128)(2,1)S(1)} copy-done((bf16[32]{0:T(256)(128)(2,1)S(1)}, bf16[32]{0:T(256)(128)(2,1)}, u32[]{:S(2)}) %copy-start.3) | copy-done | bytes 88
  2.5 30.2 %shard_map.46 = (bf16[2,2,256,1536]{3,2,1,0:T(8,128)(2,1)S(1)}, bf16[2,256,1536]{2,1,0:T(8,128)(2,1)S(1)}, bf16[256,128]{1,0:T(8,128)(2,1)S(1)}, bf16[1536,32]{1,0:T(8,128)(2,1)S(1)}, f32[2,8,768]{2,1,0:T(8,128)S(1)}) custom-call(bf16[2,32,768]{2,1,0:T(8,128)(2,1)S(1)} %copy-done.1, bf16[1,32]{1,0:T(2,128)(2,1)S(1)} %bitcast.1, s32[8,12288]{1,0:T(8,128)S(1)} %copy-done), custom_call_target="tpu_custom_call" | custom-call | tf_op jit(solution)/shard_map/pallas_call | solution.py:304
  32.8 0.0 copy-start.2
  32.8 0.7 %copy-done.2 = s32[8,96]{1,0:T(8,128)S(1)} copy-done((s32[8,96]{1,0:T(8,128)S(1)}, s32[8,96]{1,0:T(8,128)}, u32[]{:S(2)}) %copy-start.2) | copy-done | bytes 3096
  33.5 28.7 %shard_map.47 = f32[2,1536,768]{2,1,0:T(8,128)} custom-call(s32[8,96]{1,0:T(8,128)S(1)} %copy-done.2, bf16[1536,32]{1,0:T(8,128)(2,1)S(1)} %get-tuple-element.10.row_turns, f32[2,8,768]{2,1,0:T(8,128)S(1)} %get-tuple-element.11.col_turns, bf16[2,2,256,1536]{3,2,1,0:T(8,128)(2,1)S(1)} %get-tuple-element.12.hop_ref, ...), custom_call_target="tpu_custom_call" | custom-call | tf_op jit(solution)/shard_map/pallas_call | solution.py:407
Async XLA Ops:
  0.0 1.0 %copy-start = (s32[8,12288]{1,0:T(8,128)S(1)}, s32[8,12288]{1,0:T(8,128)}, u32[]{:S(2)}) copy-start(s32[8,12288]{1,0:T(8,128)} %phase_ref.1) | copy-start | bytes 1179652
  1.0 0.9 %copy-start.1 = (bf16[2,32,768]{2,1,0:T(8,128)(2,1)S(1)}, bf16[2,32,768]{2,1,0:T(8,128)(2,1)}, u32[]{:S(2)}) copy-start(bf16[2,32,768]{2,1,0:T(8,128)(2,1)} %d_ref.1) | copy-start | bytes 294916
  1.9 0.7 %copy-start.3 = (bf16[32]{0:T(256)(128)(2,1)S(1)}, bf16[32]{0:T(256)(128)(2,1)}, u32[]{:S(2)}) copy-start(bf16[32]{0:T(256)(128)(2,1)} %param.5) | copy-start | bytes 196
  32.8 0.7 %copy-start.2 = (s32[8,96]{1,0:T(8,128)S(1)}, s32[8,96]{1,0:T(8,128)}, u32[]{:S(2)}) copy-start(s32[8,96]{1,0:T(8,128)} %perm_ref.1) | copy-start | bytes 9220

commit v3 on v2

--- a/solution.py
+++ b/solution.py
@@ -16,7 +16,7 @@
 GROUP = 1536
 GROUP_BLOCKS = 12
 COL_BLOCKS = 6
-FAR_LAG = 2
+FAR_LAG = 3
 GATHER_VMEM = 16 * 2**20
 NORM = -1.0 / math.sqrt(NS * PAIRS)
 HALF_ROOT = math.sqrt(0.5)

time: 62.4 us -> 62.4 us (level)
  no operation moved by 1% of the time
where the time goes in v3:
time: 62.4 us; the launch traced here: 62.2 us
  Pallas kernels  58.9 us (94%)
  local copies, waits for them, and re-layouts  3.22 us (5%)
    pallas_call x1, Pallas kernels, gather(): pl.pallas_call(gather_kernel, out_shape=[jax.ShapeDtypeStruct((2, 2, PAIR...  30.2 us
    pallas_call x1, Pallas kernels, symmetrize(): pl.pallas_call(symmetrize_kernel, grid=(GROUP_BLOCKS,), out_shape=jax.Sha...  28.7 us
    unnamed x8, local copies, waits for them, and re-layouts  3.22 us

profile of v3, /device:TPU:1, one launch (start us, length us, event | category | flops | bytes accessed | tf_op | source)
XLA Modules:
  0.0 62.2 jit_solution(2901500311076589471)
XLA Ops:
  0.0 0.0 copy-start
  0.0 1.0 %copy-done = s32[8,12288]{1,0:T(8,128)S(1)} copy-done((s32[8,12288]{1,0:T(8,128)S(1)}, s32[8,12288]{1,0:T(8,128)}, u32[]{:S(2)}) %copy-start) | copy-done | bytes 393240
  1.0 0.0 copy-start.1
  1.0 0.9 %copy-done.1 = bf16[2,32,768]{2,1,0:T(8,128)(2,1)S(1)} copy-done((bf16[2,32,768]{2,1,0:T(8,128)(2,1)S(1)}, bf16[2,32,768]{2,1,0:T(8,128)(2,1)}, u32[]{:S(2)}) %copy-start.1) | copy-done | bytes 98328
  1.9 0.0 copy-start.3
  1.9 0.7 %copy-done.3 = bf16[32]{0:T(256)(128)(2,1)S(1)} copy-done((bf16[32]{0:T(256)(128)(2,1)S(1)}, bf16[32]{0:T(256)(128)(2,1)}, u32[]{:S(2)}) %copy-start.3) | copy-done | bytes 88
  2.5 30.2 %shard_map.46 = (bf16[2,2,256,1536]{3,2,1,0:T(8,128)(2,1)S(1)}, bf16[2,256,1536]{2,1,0:T(8,128)(2,1)S(1)}, bf16[256,128]{1,0:T(8,128)(2,1)S(1)}, bf16[1536,32]{1,0:T(8,128)(2,1)S(1)}, f32[2,8,768]{2,1,0:T(8,128)S(1)}) custom-call(bf16[2,32,768]{2,1,0:T(8,128)(2,1)S(1)} %copy-done.1, bf16[1,32]{1,0:T(2,128)(2,1)S(1)} %bitcast.1, s32[8,12288]{1,0:T(8,128)S(1)} %copy-done), custom_call_target="tpu_custom_call" | custom-call | tf_op jit(solution)/shard_map/pallas_call | solution.py:304
  32.8 0.0 copy-start.2
  32.8 0.7 %copy-done.2 = s32[8,96]{1,0:T(8,128)S(1)} copy-done((s32[8,96]{1,0:T(8,128)S(1)}, s32[8,96]{1,0:T(8,128)}, u32[]{:S(2)}) %copy-start.2) | copy-done | bytes 3096
  33.5 28.7 %shard_map.47 = f32[2,1536,768]{2,1,0:T(8,128)} custom-call(s32[8,96]{1,0:T(8,128)S(1)} %copy-done.2, bf16[1536,32]{1,0:T(8,128)(2,1)S(1)} %get-tuple-element.10.row_turns, f32[2,8,768]{2,1,0:T(8,128)S(1)} %get-tuple-element.11.col_turns, bf16[2,2,256,1536]{3,2,1,0:T(8,128)(2,1)S(1)} %get-tuple-element.12.hop_ref, ...), custom_call_target="tpu_custom_call" | custom-call | tf_op jit(solution)/shard_map/pallas_call | solution.py:407
Async XLA Ops:
  0.0 1.0 %copy-start = (s32[8,12288]{1,0:T(8,128)S(1)}, s32[8,12288]{1,0:T(8,128)}, u32[]{:S(2)}) copy-start(s32[8,12288]{1,0:T(8,128)} %phase_ref.1) | copy-start | bytes 1179652
  1.0 0.9 %copy-start.1 = (bf16[2,32,768]{2,1,0:T(8,128)(2,1)S(1)}, bf16[2,32,768]{2,1,0:T(8,128)(2,1)}, u32[]{:S(2)}) copy-start(bf16[2,32,768]{2,1,0:T(8,128)(2,1)} %d_ref.1) | copy-start | bytes 294916
  1.9 0.7 %copy-start.3 = (bf16[32]{0:T(256)(128)(2,1)S(1)}, bf16[32]{0:T(256)(128)(2,1)}, u32[]{:S(2)}) copy-start(bf16[32]{0:T(256)(128)(2,1)} %param.5) | copy-start | bytes 196
  32.8 0.7 %copy-start.2 = (s32[8,96]{1,0:T(8,128)S(1)}, s32[8,96]{1,0:T(8,128)}, u32[]{:S(2)}) copy-start(s32[8,96]{1,0:T(8,128)} %perm_ref.1) | copy-start | bytes 9220

commit v4 on v3

--- a/solution.py
+++ b/solution.py
@@ -167,8 +167,8 @@
         def _():
             cross(yy, zz, 1, from_col).start()
 
-    def cross_both(yy, zz):
-        return copy(c_at(yy, zz), r_at(q, yy, zz), cross_send.at[0], far_recv.at[2 * yy + zz], to_cross)
+    def cross_both(yy, zz, src):
+        return copy(src, r_at(q, yy, zz), cross_send.at[0], far_recv.at[2 * yy + zz], to_cross)
 
     def sib_r(yy, zz):
         return copy(r_at(q, yy, zz), r_at(q, yy, zz), sib_send.at[1], sib_recv.at[4], to_sib)
@@ -182,7 +182,7 @@
             if n % 4 != 0:
                 c_copy(yy, zz, to_zo).wait_recv()
             if n % 4 == 2:
-                cross_both(yy, zz).start()
+                cross_both(yy, zz, c_at(yy, zz)).start()
             else:
                 cross_start(yy, zz, True)
             if n > 4:
@@ -191,7 +191,10 @@
         @pl.when(jnp.logical_not(is_root))
         def _():
             copy(r_at(q, yy, zz), r_at(q, yy, zz), bulk.at[0], line_recv.at[2 * yy + zz], to_zo).wait_recv()
-            cross_start(yy, zz, False)
+            if n % 4 == 2:
+                cross_both(yy, zz, r_at(q, yy, zz)).start()
+            else:
+                cross_start(yy, zz, False)
 
             @pl.when(jnp.logical_not(on_line))
             def _():
@@ -212,12 +215,12 @@
 
         relayed = jnp.logical_not(on_line)
         if n % 4 == 2:
-            @pl.when(jnp.logical_and(relayed, is_root))
+            @pl.when(relayed)
             def _():
                 there = hop_ref.at[k, :, pair_of(yy), cols_of(zz)]
                 copy(there, there, mate_send.at[0], far_recv.at[2 * yy + zz], to_zo).wait_recv()
 
-            relayed = jnp.logical_and(relayed, jnp.logical_not(is_root))
+            return
 
         @pl.when(jnp.logical_and(relayed, zp == 0))
         def _():
@@ -245,7 +248,6 @@
         sib_c(yy, 1 - k).wait_recv()
 
     half = hop_ref.at[k, :, 0:PAIRS // 2, :]
-    whole = hop_ref.at[k, 0]
     most = hop_ref.at[k, 0, 0:3 * PAIRS // 4, :]
     far_root = jnp.logical_and(jnp.logical_not(on_line), is_root)
     far_other = jnp.logical_and(jnp.logical_not(on_line), jnp.logical_not(is_root))
@@ -256,7 +258,7 @@
 
     @pl.when(far_other)
     def _():
-        copy(whole, whole, mate_send.at[0], mate_recv.at[0], to_zo).wait_recv()
+        copy(most, most, mate_send.at[0], mate_recv.at[0], to_zo).wait_recv()
 
     @pl.when(jnp.logical_and(on_line, jnp.logical_not(is_root)))
     def _():
@@ -273,7 +275,6 @@
     sent = col_ref.at[:, 0:208, :]
     copy(sent, sent, bulk.at[0], c_recv.at[0], to_zo).wait_send()
     copy(half, half, sib_send.at[0], sib_recv.at[0], to_sib).wait_send()
-    part_half = hop_ref.at[k, 0, 0:PAIRS // 2, :]
     part_more = hop_ref.at[k, 0, 0:5 * PAIRS // 8, :]
 
     @pl.when(is_root)
@@ -282,7 +283,7 @@
 
     @pl.when(jnp.logical_not(is_root))
     def _():
-        copy(part_half, part_half, cross_send.at[0], far_recv.at[0], to_zo).wait_send()
+        copy(part_more, part_more, cross_send.at[0], far_recv.at[0], to_zo).wait_send()
 
     w_sent = wt_ref.at[0:7 * SHARE, :]
     copy(w_sent, w_sent, w_send.at[0], w_recv.at[0], to_sib).wait_send()
@@ -293,7 +294,7 @@
 
     @pl.when(far_other)
     def _():
-        copy(whole, whole, mate_send.at[0], mate_recv.at[0], to_zo).wait_send()
+        copy(most, most, mate_send.at[0], mate_recv.at[0], to_zo).wait_send()
         copy(half, half, sib_send.at[1], sib_recv.at[4], to_sib).wait_send()
 
 
@@ -325,7 +326,7 @@
 
 def symmetrize_kernel(
     perm_ref, row_turns, col_turns, hop_ref, col_ref, wt_ref, out_ref,
-    chi, left, right, spread, turns, col_cos, col_sin,
+    chi, left, spread, turns, col_cos, col_sin,
 ):
     row = lax.axis_index("row")
     col = lax.axis_index("col")
@@ -350,21 +351,23 @@
             tile = pl.ds(pl.multiple_of(t * BLOCK, BLOCK), BLOCK)
             for part in range(2):
                 scaled = hop_ref[row % 2, part, :, tile].astype(jnp.float32) * weight
-                left[tile, part * PAIRS:(part + 1) * PAIRS] = scaled.T.astype(jnp.bfloat16)
+                turned = scaled.astype(jnp.bfloat16).T
+                left[tile, part * PAIRS:(part + 1) * PAIRS] = turned
+                if part == 0:
+                    left[tile, 2 * PAIRS:3 * PAIRS] = -turned
             return c
 
-        lax.fori_loop(0, GROUP_BLOCKS, prepare_left, 0, unroll=6)
-        right[0:PAIRS, 0:GROUP] = col_ref[0]
-        right[PAIRS:2 * PAIRS, 0:GROUP] = col_ref[1]
-        right[0:PAIRS, GROUP:2 * GROUP] = -col_ref[1]
-        right[PAIRS:2 * PAIRS, GROUP:2 * GROUP] = col_ref[0]
+        lax.fori_loop(0, GROUP_BLOCKS, prepare_left, 0, unroll=12)
+        right = col_ref[...].reshape(2 * PAIRS, GROUP)
 
         def multiply(up, c):
             rows = pl.ds(pl.multiple_of(up * 768, 768), 768)
-            tile = jnp.dot(left[rows, :], right[...], preferred_element_type=jnp.float32)
-            for i in range(6):
-                for j in range(2 * GROUP_BLOCKS):
-                    chi[up * 6 + i, j] = tile[i * BLOCK:(i + 1) * BLOCK, j * BLOCK:(j + 1) * BLOCK]
+            for part in range(2):
+                pieces = left[rows, part * PAIRS:(part + 2) * PAIRS]
+                tile = jnp.dot(pieces, right, preferred_element_type=jnp.float32)
+                for i in range(6):
+                    for j in range(GROUP_BLOCKS):
+                        chi[up * 6 + i, part * GROUP_BLOCKS + j] = tile[i * BLOCK:(i + 1) * BLOCK, j * BLOCK:(j + 1) * BLOCK]
             return c
 
         lax.fori_loop(0, 2, multiply, 0)
@@ -412,8 +415,7 @@
         out_specs=pl.BlockSpec((2, BLOCK, WIDE), lambda b: (0, b, 0)),
         scratch_shapes=[
             pltpu.VMEM((GROUP_BLOCKS, 2 * GROUP_BLOCKS, BLOCK, BLOCK), f32),
-            pltpu.VMEM((GROUP, 2 * PAIRS), bf16),
-            pltpu.VMEM((2 * PAIRS, 2 * GROUP), bf16),
+            pltpu.VMEM((GROUP, 3 * PAIRS), bf16),
             pltpu.VMEM((4 * NS, 2 * NS * BLOCK), bf16),
             pltpu.VMEM((BLOCK, 2 * NS * BLOCK), f32),
             pltpu.VMEM((NS, COL_BLOCKS, 8, BLOCK), f32),

time: 62.4 us -> 62.1 us (level)
  no operation moved by 1% of the time
where the time goes in v4:
time: 62.1 us; the launch traced here: 61.9 us
  Pallas kernels  58.7 us (95%)
  local copies, waits for them, and re-layouts  3.22 us (5%)
    pallas_call x1, Pallas kernels, gather(): pl.pallas_call(gather_kernel, out_shape=[jax.ShapeDtypeStruct((2, 2, PAIR...  30.2 us
    pallas_call x1, Pallas kernels, symmetrize(): pl.pallas_call(symmetrize_kernel, grid=(GROUP_BLOCKS,), out_shape=jax.Sha...  28.4 us
    unnamed x8, local copies, waits for them, and re-layouts  3.22 us

profile of v4, /device:TPU:1, one launch (start us, length us, event | category | flops | bytes accessed | tf_op | source)
XLA Modules:
  0.0 61.9 jit_solution(16591808042311321220)
XLA Ops:
  0.0 0.0 copy-start
  0.0 1.0 %copy-done = s32[8,12288]{1,0:T(8,128)S(1)} copy-done((s32[8,12288]{1,0:T(8,128)S(1)}, s32[8,12288]{1,0:T(8,128)}, u32[]{:S(2)}) %copy-start) | copy-done | bytes 393240
  1.0 0.0 copy-start.1
  1.0 0.9 %copy-done.1 = bf16[2,32,768]{2,1,0:T(8,128)(2,1)S(1)} copy-done((bf16[2,32,768]{2,1,0:T(8,128)(2,1)S(1)}, bf16[2,32,768]{2,1,0:T(8,128)(2,1)}, u32[]{:S(2)}) %copy-start.1) | copy-done | bytes 98328
  1.9 0.0 copy-start.3
  1.9 0.7 %copy-done.3 = bf16[32]{0:T(256)(128)(2,1)S(1)} copy-done((bf16[32]{0:T(256)(128)(2,1)S(1)}, bf16[32]{0:T(256)(128)(2,1)}, u32[]{:S(2)}) %copy-start.3) | copy-done | bytes 88
  2.5 30.2 %shard_map.46 = (bf16[2,2,256,1536]{3,2,1,0:T(8,128)(2,1)S(1)}, bf16[2,256,1536]{2,1,0:T(8,128)(2,1)S(1)}, bf16[256,128]{1,0:T(8,128)(2,1)S(1)}, bf16[1536,32]{1,0:T(8,128)(2,1)S(1)}, f32[2,8,768]{2,1,0:T(8,128)S(1)}) custom-call(bf16[2,32,768]{2,1,0:T(8,128)(2,1)S(1)} %copy-done.1, bf16[1,32]{1,0:T(2,128)(2,1)S(1)} %bitcast.1, s32[8,12288]{1,0:T(8,128)S(1)} %copy-done), custom_call_target="tpu_custom_call" | custom-call | tf_op jit(solution)/shard_map/pallas_call | solution.py:305
  32.8 0.0 copy-start.2
  32.8 0.7 %copy-done.2 = s32[8,96]{1,0:T(8,128)S(1)} copy-done((s32[8,96]{1,0:T(8,128)S(1)}, s32[8,96]{1,0:T(8,128)}, u32[]{:S(2)}) %copy-start.2) | copy-done | bytes 3096
  33.5 28.4 %shard_map.47 = f32[2,1536,768]{2,1,0:T(8,128)} custom-call(s32[8,96]{1,0:T(8,128)S(1)} %copy-done.2, bf16[1536,32]{1,0:T(8,128)(2,1)S(1)} %get-tuple-element.10.row_turns, f32[2,8,768]{2,1,0:T(8,128)S(1)} %get-tuple-element.11.col_turns, bf16[2,2,256,1536]{3,2,1,0:T(8,128)(2,1)S(1)} %get-tuple-element.12.hop_ref, ...), custom_call_target="tpu_custom_call" | custom-call | tf_op jit(solution)/shard_map/pallas_call | solution.py:410
Async XLA Ops:
  0.0 1.0 %copy-start = (s32[8,12288]{1,0:T(8,128)S(1)}, s32[8,12288]{1,0:T(8,128)}, u32[]{:S(2)}) copy-start(s32[8,12288]{1,0:T(8,128)} %phase_ref.1) | copy-start | bytes 1179652
  1.0 0.9 %copy-start.1 = (bf16[2,32,768]{2,1,0:T(8,128)(2,1)S(1)}, bf16[2,32,768]{2,1,0:T(8,128)(2,1)}, u32[]{:S(2)}) copy-start(bf16[2,32,768]{2,1,0:T(8,128)(2,1)} %d_ref.1) | copy-start | bytes 294916
  1.9 0.7 %copy-start.3 = (bf16[32]{0:T(256)(128)(2,1)S(1)}, bf16[32]{0:T(256)(128)(2,1)}, u32[]{:S(2)}) copy-start(bf16[32]{0:T(256)(128)(2,1)} %param.5) | copy-start | bytes 196
  32.8 0.7 %copy-start.2 = (s32[8,96]{1,0:T(8,128)S(1)}, s32[8,96]{1,0:T(8,128)}, u32[]{:S(2)}) copy-start(s32[8,96]{1,0:T(8,128)} %perm_ref.1) | copy-start | bytes 9220

commit v5 on v4

--- a/solution.py
+++ b/solution.py
@@ -116,6 +116,16 @@
     c_copy(y, zp, to_zo, d_ref).start()
     spread_block(zp, d_ref)
 
+    keep.wait()
+    c_copy(y, 1 - zp, to_zo).wait_recv()
+    spread_block(1 - zp, c_at(y, 1 - zp))
+
+    def sib_c(yy, kk):
+        there = col_ref.at[:, rows_of(yy, kk), :]
+        return copy(there, there, sib_send.at[0], sib_recv.at[yy], to_sib)
+
+    sib_c(y, k).start()
+
     cosine, sine = turn_parts(phase_ref[:, pl.ds(pl.multiple_of(col * WIDE, BLOCK), WIDE)])
     col_turns[0] = cosine
     col_turns[1] = sine
@@ -129,15 +139,6 @@
         return carry
 
     lax.fori_loop(0, GROUP_BLOCKS, row_block, 0)
-    keep.wait()
-    c_copy(y, 1 - zp, to_zo).wait_recv()
-    spread_block(1 - zp, c_at(y, 1 - zp))
-
-    def sib_c(yy, kk):
-        there = col_ref.at[:, rows_of(yy, kk), :]
-        return copy(there, there, sib_send.at[0], sib_recv.at[yy], to_sib)
-
-    sib_c(y, k).start()
 
     get_w.wait()
     lanes = lax.broadcasted_iota(jnp.int32, (SHARE, SHARE), 1)

time: 62.1 us -> 62.1 us (level)
  no operation moved by 1% of the time
where the time goes in v5:
time: 62.1 us; the launch traced here: 61.9 us
  Pallas kernels  58.7 us (95%)
  local copies, waits for them, and re-layouts  3.22 us (5%)
    pallas_call x1, Pallas kernels, gather(): pl.pallas_call(gather_kernel, out_shape=[jax.ShapeDtypeStruct((2, 2, PAIR...  30.2 us
    pallas_call x1, Pallas kernels, symmetrize(): pl.pallas_call(symmetrize_kernel, grid=(GROUP_BLOCKS,), out_shape=jax.Sha...  28.4 us
    unnamed x8, local copies, waits for them, and re-layouts  3.22 us

profile of v5, /device:TPU:1, one launch (start us, length us, event | category | flops | bytes accessed | tf_op | source)
XLA Modules:
  0.0 61.9 jit_solution(10074471355295384267)
XLA Ops:
  0.0 0.0 copy-start
  0.0 1.0 %copy-done = s32[8,12288]{1,0:T(8,128)S(1)} copy-done((s32[8,12288]{1,0:T(8,128)S(1)}, s32[8,12288]{1,0:T(8,128)}, u32[]{:S(2)}) %copy-start) | copy-done | bytes 393240
  1.0 0.0 copy-start.1
  1.0 0.9 %copy-done.1 = bf16[2,32,768]{2,1,0:T(8,128)(2,1)S(1)} copy-done((bf16[2,32,768]{2,1,0:T(8,128)(2,1)S(1)}, bf16[2,32,768]{2,1,0:T(8,128)(2,1)}, u32[]{:S(2)}) %copy-start.1) | copy-done | bytes 98328
  1.9 0.0 copy-start.3
  1.9 0.7 %copy-done.3 = bf16[32]{0:T(256)(128)(2,1)S(1)} copy-done((bf16[32]{0:T(256)(128)(2,1)S(1)}, bf16[32]{0:T(256)(128)(2,1)}, u32[]{:S(2)}) %copy-start.3) | copy-done | bytes 88
  2.5 30.2 %shard_map.46 = (bf16[2,2,256,1536]{3,2,1,0:T(8,128)(2,1)S(1)}, bf16[2,256,1536]{2,1,0:T(8,128)(2,1)S(1)}, bf16[256,128]{1,0:T(8,128)(2,1)S(1)}, bf16[1536,32]{1,0:T(8,128)(2,1)S(1)}, f32[2,8,768]{2,1,0:T(8,128)S(1)}) custom-call(bf16[2,32,768]{2,1,0:T(8,128)(2,1)S(1)} %copy-done.1, bf16[1,32]{1,0:T(2,128)(2,1)S(1)} %bitcast.1, s32[8,12288]{1,0:T(8,128)S(1)} %copy-done), custom_call_target="tpu_custom_call" | custom-call | tf_op jit(solution)/shard_map/pallas_call | solution.py:306
  32.8 0.0 copy-start.2
  32.8 0.7 %copy-done.2 = s32[8,96]{1,0:T(8,128)S(1)} copy-done((s32[8,96]{1,0:T(8,128)S(1)}, s32[8,96]{1,0:T(8,128)}, u32[]{:S(2)}) %copy-start.2) | copy-done | bytes 3096
  33.5 28.4 %shard_map.47 = f32[2,1536,768]{2,1,0:T(8,128)} custom-call(s32[8,96]{1,0:T(8,128)S(1)} %copy-done.2, bf16[1536,32]{1,0:T(8,128)(2,1)S(1)} %get-tuple-element.10.row_turns, f32[2,8,768]{2,1,0:T(8,128)S(1)} %get-tuple-element.11.col_turns, bf16[2,2,256,1536]{3,2,1,0:T(8,128)(2,1)S(1)} %get-tuple-element.12.hop_ref, ...), custom_call_target="tpu_custom_call" | custom-call | tf_op jit(solution)/shard_map/pallas_call | solution.py:411
Async XLA Ops:
  0.0 1.0 %copy-start = (s32[8,12288]{1,0:T(8,128)S(1)}, s32[8,12288]{1,0:T(8,128)}, u32[]{:S(2)}) copy-start(s32[8,12288]{1,0:T(8,128)} %phase_ref.1) | copy-start | bytes 1179652
  1.0 0.9 %copy-start.1 = (bf16[2,32,768]{2,1,0:T(8,128)(2,1)S(1)}, bf16[2,32,768]{2,1,0:T(8,128)(2,1)}, u32[]{:S(2)}) copy-start(bf16[2,32,768]{2,1,0:T(8,128)(2,1)} %d_ref.1) | copy-start | bytes 294916
  1.9 0.7 %copy-start.3 = (bf16[32]{0:T(256)(128)(2,1)S(1)}, bf16[32]{0:T(256)(128)(2,1)}, u32[]{:S(2)}) copy-start(bf16[32]{0:T(256)(128)(2,1)} %param.5) | copy-start | bytes 196
  32.8 0.7 %copy-start.2 = (s32[8,96]{1,0:T(8,128)S(1)}, s32[8,96]{1,0:T(8,128)}, u32[]{:S(2)}) copy-start(s32[8,96]{1,0:T(8,128)} %perm_ref.1) | copy-start | bytes 9220
